TPU v7x, 32 devices: a whole 2x2x4 slice. The times are simulated.
32 devices in a mesh: groups: 2 (over y), tm: 16 (over z, x, core).
Axes of the slice: x: 2, y: 2, z: 4, core: 2. Of those that a mesh axis runs over, the one named last changes fastest.
Arguments:
- video: bfloat16 [32, 384, 1152], P(('groups', 'tm')), parts along dimension 0, may hold values from -6 to 6
- cam_len: int32 [32, 6], P(('groups', 'tm')), parts along dimension 0, may hold values from 16 to 64, as said below
- view_mask: int32 [6, 6], replicated, may hold values 0 or 1
- time_mask: int32 [8, 8], replicated, may hold values 0 or 1
- s_gain: float32 [1152], replicated, may hold values from 0.4 to 1.6
- t_gain: float32 [1152], replicated, may hold values from 0.4 to 1.6
- s_qkv: bfloat16 [1152, 1728], replicated, may hold values from -0.1875 to 0.1875
- s_out: bfloat16 [576, 1152], replicated, may hold values from -0.25 to 0.25
- t_qkv: bfloat16 [1152, 1728], replicated, may hold values from -0.1875 to 0.1875
- t_out: bfloat16 [576, 1152], replicated, may hold values from -0.25 to 0.25
- qk_gain: float32 [4, 72], replicated, as said below
Outputs:
- result: bfloat16 [32, 384, 1152], P(('groups', 'tm')), parts along dimension 0
There are 2 independent parts, one for each index of `groups`. A program takes and returns all parts, laid end to end along the dimension named above; an argument that names none is the same for every part. Nothing has to cross between parts.
Inputs may be any that keep to these rules, and one draw needn't show every extreme that they name: `cam_len`: every frame has a camera with exactly 64 live tokens. `qk_gain`: positive gains.
All inputs are finite; a program needn't handle non-finite values.
Results may differ from a plain program's by a relative error of at most 0.02.
The roundings to bfloat16 on the way count: a program that leaves them out, or rounds other values in their place, can miss the bound.
Values may be sent and summed in bfloat16 or wider, within the bound.
A program may use at most 64 MiB of HBM per device.

v0:
```python
import jax
import jax.numpy as jnp
from jax import lax
from jax.sharding import PartitionSpec as P

HEADS = 8
HD = 72
CAMS = 6
NBLK = 8


epsilon = 1e-06


def layer_norm(features, norm_gain):
    values_f = features.astype(jnp.float32)
    average = jnp.mean(values_f, -1, keepdims=True)
    centred = values_f - average
    spread = jnp.mean(centred * centred, -1, keepdims=True)
    return (centred * lax.rsqrt(spread + epsilon) * norm_gain).astype(jnp.bfloat16)


def qkv_heads(normed, matrix, qk_gains):
    leading = normed.shape[:-1]
    projected = jnp.dot(
        normed.reshape(-1, normed.shape[-1]), matrix, preferred_element_type=jnp.float32
    )
    projected = projected.reshape((-1, 3, HEADS, HD))
    queries = projected[:, 0]
    keys_part = projected[:, 1]
    values_part = projected[:, 2]
    queries = (
        queries * lax.rsqrt(jnp.mean(queries * queries, -1, keepdims=True) + epsilon) * qk_gains[0]
    )
    keys_part = (
        keys_part
        * lax.rsqrt(jnp.mean(keys_part * keys_part, -1, keepdims=True) + epsilon)
        * qk_gains[1]
    )
    packed = jnp.stack([queries, keys_part, values_part], 1).astype(jnp.bfloat16)
    return packed.reshape(leading + (3 * HEADS * HD,))


def softmax_rows(scores):
    highest = jnp.max(scores, -1, keepdims=True)
    exponent = jnp.exp(scores - highest)
    return (exponent / jnp.sum(exponent, -1, keepdims=True)).astype(jnp.bfloat16)


def spatial_frame(this_frame, lengths, view_mask, norm_gain, w_qkv, w_out, qk_gains):
    token_rows = this_frame.shape[0]
    tile_rows = token_rows // CAMS
    packed = qkv_heads(layer_norm(this_frame, norm_gain), w_qkv, qk_gains).reshape(
        token_rows, 3, HEADS, HD
    )
    ordinal = jnp.arange(token_rows, dtype=jnp.int32)
    camera = ordinal // tile_rows
    position = ordinal % tile_rows
    onehot = (camera[:, None] == jnp.arange(CAMS, dtype=jnp.int32)[None, :]).astype(jnp.float32)
    lengths_here = jnp.sum(onehot * lengths.astype(jnp.float32)[None, :], 1)
    usable = position.astype(jnp.float32) < lengths_here
    linked = jnp.dot(
        jnp.dot(onehot, view_mask.astype(jnp.float32), precision=lax.Precision.HIGHEST),
        onehot.T,
        precision=lax.Precision.HIGHEST,
    )
    allowed = ((linked > 0.5) | (camera[:, None] == camera[None, :])) & usable[None, :]
    scores = jnp.einsum(
        "qhd,khd->hqk", packed[:, 0], packed[:, 1], preferred_element_type=jnp.float32
    ) * HD ** (-0.5)
    scores = jnp.where(allowed[None], scores, -1e30)
    weights = softmax_rows(scores)
    attended = jnp.einsum("hqk,khd->qhd", weights, packed[:, 2], preferred_element_type=jnp.float32)
    attended = attended.astype(jnp.bfloat16).reshape(token_rows, HEADS * HD)
    projected = jnp.dot(attended, w_out, preferred_element_type=jnp.float32)
    after_space = (this_frame.astype(jnp.float32) + projected).astype(jnp.bfloat16)
    return (after_space, usable)


def frame_links(time_mask, frames):
    block_len = frames // NBLK
    expanded = jnp.repeat(jnp.repeat(time_mask, block_len, 0), block_len, 1) > 0
    ordinal = jnp.arange(frames, dtype=jnp.int32)
    earlier = ordinal[:, None] > ordinal[None, :]
    return expanded & earlier


def temporal_block(packed, usable, links):
    frames, item_count = (packed.shape[0], packed.shape[1])
    pieces = packed.reshape(frames, item_count, 3, HEADS, HD)
    scores = jnp.einsum(
        "fmhd,gmhd->mhfg", pieces[:, :, 0], pieces[:, :, 1], preferred_element_type=jnp.float32
    ) * HD ** (-0.5)
    ordinal = jnp.arange(frames, dtype=jnp.int32)
    diagonal = ordinal[:, None] == ordinal[None, :]
    allowed = diagonal[None] | links[None] & usable.T[:, None, :]
    scores = jnp.where(allowed[:, None], scores, -1e30)
    weights = softmax_rows(scores)
    attended = jnp.einsum(
        "mhfg,gmhd->fmhd", weights, pieces[:, :, 2], preferred_element_type=jnp.float32
    )
    return attended.astype(jnp.bfloat16).reshape(frames, item_count, HEADS * HD)


def body(video, cam_len, view_mask, time_mask, s_gain, t_gain, s_qkv, s_out, t_qkv, t_out, qk_gain):
    this_frame = video[0]
    token_rows, model_width = this_frame.shape
    after_space, usable = spatial_frame(
        this_frame, cam_len[0], view_mask, s_gain, s_qkv, s_out, qk_gain[0:2]
    )
    normed = layer_norm(after_space, t_gain)
    members = lax.axis_size("tm")
    per_peer = token_rows // members
    usable_marks = usable.astype(jnp.bfloat16).reshape(members, per_peer)
    links = frame_links(time_mask, members)
    packed = qkv_heads(
        lax.all_to_all(
            normed.reshape(members, per_peer, model_width),
            "tm",
            split_axis=0,
            concat_axis=0,
            tiled=True,
        ),
        t_qkv,
        qk_gain[2:4],
    )
    attended = temporal_block(
        packed,
        lax.all_to_all(usable_marks, "tm", split_axis=0, concat_axis=0, tiled=True) > 0.5,
        links,
    )
    gathered = lax.all_to_all(attended, "tm", split_axis=0, concat_axis=0, tiled=True)
    merged = gathered.reshape(token_rows, -1)
    projected = jnp.dot(merged, t_out, preferred_element_type=jnp.float32).astype(jnp.bfloat16)
    result = (after_space.astype(jnp.float32) + projected.astype(jnp.float32)).astype(jnp.bfloat16)
    return result[None]


def solution(mesh):
    placed = (
        P(("groups", "tm"), None, None),
        P(("groups", "tm"), None),
        P(),
        P(),
        P(),
        P(),
        P(),
        P(),
        P(),
        P(),
        P(),
    )
    return jax.shard_map(
        body, mesh=mesh, in_specs=placed, out_specs=P(("groups", "tm"), None, None), check_vma=False
    )
```

profile of v0, /device:TPU:0, one launch (start us, length us, event | category | flops | bytes accessed | tf_op | source)
XLA Modules:
  0.0 103.6 jit_solution(10694934743971508109)
XLA Ops:
  0.0 0.0 copy-start
  0.0 0.0 copy-start.1
  0.0 0.0 copy-start.7
  0.0 0.8 convert_bitcast_fusion.1
  0.8 0.1 select_reduce_fusion
  0.9 0.1 reduce_sum.109
  1.0 0.6 copy.62
  1.6 7.4 %all-to-all-start.1 = ((bf16[16,1,24]{2,1,0:T(2,128)(2,1)}), bf16[16,1,24]{2,1,0:T(2,128)(2,1)S(1)}, u32[]{:S(2)}, u32[]{:S(2)}) async-start(bf16[16,1,24]{2,1,0:T(2,128)(2,1)} %copy.62), calls=%async_computation.1 | async-start | bytes 16384 | tf_op jit(solution)/shard_map/all_to_all | solution.py:129
  9.0 1.4 %convert_reduce_fusion = f32[384]{0:T(512)S(1)} fusion(bf16[1,384,1152]{2,1,0:T(8,128)(2,1)} %param.11), kind=kLoop, calls=%fused_computation.14 | loop fusion | flops 884352 | bytes 886272 | tf_op jit(solution)/shard_map/reduce_sum | solution.py:17
  10.4 1.5 %fusion.15 = f32[384]{0:T(512)S(1)} fusion(bf16[1,384,1152]{2,1,0:T(8,128)(2,1)} %param.11, f32[384]{0:T(512)S(1)} %broadcast_multiply_fusion.1), kind=kLoop, calls=%fused_computation.23 | loop fusion | flops 1769088 | bytes 887808 | tf_op jit(solution)/shard_map/reduce_sum | solution.py:19
  11.9 0.0 copy-done.1
  11.9 0.0 copy-done.7
  11.9 4.8 %fusion.26 = f32[384,3,8,72]{0,3,2,1:T(8,128)S(1)} fusion(bf16[3,8,72,1152]{3,2,1,0:T(8,128)(2,1)} %bitcast.95, bf16[1,384,1152]{2,1,0:T(8,128)(2,1)S(1)} %copy-done.1, f32[1152]{0:T(1024)S(1)} %copy-done.7, f32[384]{0:T(512)S(1)} %add_rsqrt_fusion.5, f32[384]{0:T(512)S(1)} %broadcast_multiply_fusion.1), kind=kOutput, calls=%fused_computation.40 | convolution fusion | flops 1531035648 | bytes 7527936 | tf_op jit(solution)/shard_map/dot_general | solution.py:25
  16.8 0.0 copy-start.3
  16.8 1.5 %copy-done.3 = f32[384,3,8,72]{0,3,2,1:T(8,128)} copy-done((f32[384,3,8,72]{0,3,2,1:T(8,128)}, f32[384,3,8,72]{0,3,2,1:T(8,128)S(1)}, u32[]{:S(2)}) %copy-start.3) | copy-done | bytes 2654232
  18.3 0.0 copy-start.8
  18.3 0.0 copy-start.6
  18.3 0.2 multiply_reduce_fusion.4
  18.5 0.5 copy-done.8
  19.0 0.2 fusion.41
  19.2 0.6 fusion.24
  19.8 0.3 copy.58
  20.1 0.0 copy-done.6
  20.1 5.4 %fusion.69 = (f32[8,384]{1,0:T(8,128)S(1)}, f32[8,384,384]{1,2,0:T(8,128)}) fusion(pred[384,384]{0,1:T(8,128)(4,1)S(1)} %copy.58, f32[384,3,8,72]{0,3,2,1:T(8,128)} %copy-done.3, f32[72]{0:T(128)S(1)} %get-tuple-element.12, f32[384,8]{0,1:T(8,128)S(1)} %get-tuple-element.21, f32[72]{0:T(128)S(1)} %get-tuple-element.13, f32[384,8]{0,1:T(8,128)S(1)} %get-tuple-element.22), kind=kOutput, calls=%fused_computation.109 | convolution fusion | flops 175915392 | bytes 6672960 | tf_op jit(solution)/shard_map/sub | solution.py:46
  25.5 0.0 copy-start.2
  25.5 3.2 %fusion.22 = bf16[8,72,384]{2,1,0:T(8,128)(2,1)S(1)} fusion(f32[8,384,384]{1,2,0:T(8,128)} %get-tuple-element.16, f32[8,384]{1,0:T(8,128)S(1)} %get-tuple-element.15, f32[384,3,8,72]{0,3,2,1:T(8,128)} %copy-done.3), kind=kOutput, calls=%fused_computation.35 | convolution fusion | flops 172449792 | bytes 5615616 | tf_op jit(solution)/shard_map/hqk,khd->qhd/dot_general | solution.py:73
  28.8 0.0 copy-done
  28.8 0.0 copy-done.2
  28.8 1.1 %fusion.78 = (f32[384]{0:T(512)S(1)}, f32[384,1152]{1,0:T(8,128)S(1)}) fusion(bf16[384,576]{0,1:T(8,128)(2,1)S(1)} %bitcast.94, bf16[576,1152]{1,0:T(8,128)(2,1)S(1)} %copy-done, bf16[1,384,1152]{2,1,0:T(8,128)(2,1)S(1)} %copy-done.2), kind=kOutput, calls=%fused_computation.110 | convolution fusion | flops 511819392 | bytes 4425216 | tf_op jit(solution)/shard_map/dot_general | solution.py:75
  29.9 0.0 copy-start.4
  29.9 0.3 multiply_reduce_fusion
  30.2 0.4 copy-done.4
  30.6 0.0 copy-start.5
  30.6 1.2 %multiply_convert_fusion = bf16[384,1152]{1,0:T(8,128)(2,1)} fusion(f32[384,1152]{1,0:T(8,128)S(1)} %get-tuple-element.18, f32[1152]{0:T(1024)S(1)} %copy-done.4, f32[384]{0:T(512)S(1)} %add_rsqrt_fusion.4, f32[384]{0:T(512)S(1)} %broadcast_multiply_fusion), kind=kLoop, calls=%fused_computation.27 | loop fusion | flops 1769472 | bytes 2661888 | tf_op jit(solution)/shard_map/convert_element_type | solution.py:20
  31.8 0.0 all-to-all-done.1
  31.8 6.1 %all-to-all-start = ((bf16[16,24,1152]{2,1,0:T(8,128)(2,1)}), bf16[16,24,1152]{2,1,0:T(8,128)(2,1)}, u32[]{:S(2)}, u32[]{:S(2)}) async-start(bf16[16,24,1152]{2,1,0:T(8,128)(2,1)} %bitcast.89), calls=%async_computation | async-start | bytes 1769472 | tf_op jit(solution)/shard_map/all_to_all | solution.py:117
  37.9 0.0 copy-done.5
  37.9 0.1 copy.61
  38.1 0.1 copy.64
  38.2 0.7 and_or_fusion
  38.9 19.3 %all-to-all-done = bf16[16,24,1152]{2,1,0:T(8,128)(2,1)} async-done(((bf16[16,24,1152]{2,1,0:T(8,128)(2,1)}), bf16[16,24,1152]{2,1,0:T(8,128)(2,1)}, u32[]{:S(2)}, u32[]{:S(2)}) %all-to-all-start) | async-done | bytes 884768 | tf_op jit(solution)/shard_map/all_to_all | solution.py:117
  58.2 5.0 %fusion.84 = f32[384,3,8,72]{0,3,2,1:T(8,128)S(1)} fusion(bf16[384,1152,1,1]{1,0,3,2:T(8,128)(2,1)} %bitcast.17, bf16[3,8,72,1152]{3,2,1,0:T(8,128)(2,1)} %bitcast.96), kind=kOutput, calls=%fused_computation.112 | convolution fusion | flops 1528823808 | bytes 7520256 | tf_op jit(solution)/shard_map/dot_general | solution.py:25
  63.2 0.2 multiply_reduce_fusion.2
  63.3 0.1 slice.109
  63.4 1.2 %multiply_convert_fusion.2 = (bf16[384,1,8,72]{0,3,2,1:T(8,128)(2,1)}, bf16[384,1,8,72]{0,3,2,1:T(8,128)(2,1)}) fusion(f32[384,3,8,72]{0,3,2,1:T(8,128)S(1)} %fusion.84, f32[72]{0:T(128)S(1)} %get-tuple-element.11, f32[384,8]{0,1:T(8,128)S(1)} %add_rsqrt_fusion.1, f32[72]{0:T(128)S(1)} %get-tuple-element.14, f32[384,8]{0,1:T(8,128)S(1)} %add_rsqrt_fusion), kind=kLoop, calls=%fused_computation.45 | loop fusion | flops 1327104 | bytes 2679360 | tf_op jit(solution)/shard_map/convert.6
  64.6 2.3 %copy.65 = bf16[384,1,8,72]{3,2,0,1:T(8,128)(2,1)} copy(bf16[384,1,8,72]{0,3,2,1:T(8,128)(2,1)} %get-tuple-element.9) | data formatting | bytes 884736 | tf_op jit(solution)/shard_map/convert.6
  67.0 2.3 %copy.66 = bf16[384,1,8,72]{3,2,0,1:T(8,128)(2,1)} copy(bf16[384,1,8,72]{0,3,2,1:T(8,128)(2,1)} %get-tuple-element.10) | data formatting | bytes 884736 | tf_op jit(solution)/shard_map/convert.5
  69.3 1.4 %copy.60 = bf16[384,1,8,72]{3,2,0,1:T(8,128)(2,1)} copy(bf16[384,1,8,72]{0,3,2,1:T(8,128)(2,1)S(1)} %slice.109) | data formatting | bytes 884736 | tf_op jit(solution)/shard_map/slice | solution.py:31
  70.7 4.1 %fusion.79 = (f32[24,8,16]{2,1,0:T(8,128)S(1)}, f32[24,8,16,16]{2,3,1,0:T(8,128)}) fusion(bf16[16,24,8,72]{3,2,1,0:T(8,128)(2,1)} %bitcast.93, bf16[16,24,8,72]{3,2,1,0:T(8,128)(2,1)} %bitcast.91, pred[24,16,16]{1,2,0:T(8,128)(4,1)} %and_or_fusion), kind=kOutput, calls=%fused_computation.111 | convolution fusion | flops 7274511 | bytes 1099776 | tf_op jit(solution)/shard_map/sub | solution.py:46
  74.7 2.3 %fusion.21 = bf16[16,24,8,72]{3,0,2,1:T(8,128)(2,1)S(1)} fusion(f32[24,8,16,16]{2,3,1,0:T(8,128)} %get-tuple-element.20, bf16[16,24,8,72]{3,2,1,0:T(8,128)(2,1)} %bitcast.92, f32[24,8,16]{2,1,0:T(8,128)S(1)} %get-tuple-element.19), kind=kOutput, calls=%fused_computation.34 | convolution fusion | flops 7397376 | bytes 1093632 | tf_op jit(solution)/shard_map/mhfg,gmhd->fmhd/dot_general | solution.py:99
  77.1 1.1 %copy.71 = bf16[16,24,8,72]{3,2,1,0:T(8,128)(2,1)} copy(bf16[16,24,8,72]{3,0,2,1:T(8,128)(2,1)S(1)} %fusion.21) | data formatting | bytes 884736 | tf_op jit(solution)/shard_map/convert_element_type | solution.py:102
  78.2 2.4 %reshape.272 = bf16[16,24,576]{2,1,0:T(8,128)(2,1)} reshape(bf16[16,24,8,72]{3,2,1,0:T(8,128)(2,1)} %copy.71) | data formatting | bytes 884736 | tf_op jit(solution)/shard_map/reshape | solution.py:102
  80.6 19.8 %all_to_all.16 = bf16[16,24,576]{2,1,0:T(8,128)(2,1)S(1)} all-to-all(bf16[16,24,576]{2,1,0:T(8,128)(2,1)} %reshape.272), channel_id=1, replica_groups=mesh['groups'=2,'tm'=16] {'tm'}, dimensions={0} | all-to-all | bytes 884736 | tf_op jit(solution)/shard_map/all_to_all | solution.py:132
  100.4 3.2 %fusion.8 = bf16[1,384,1152]{2,1,0:T(8,128)(2,1)} fusion(f32[384,1152]{1,0:T(8,128)S(1)} %get-tuple-element.18, bf16[384,576]{1,0:T(8,128)(2,1)S(1)} %bitcast.90, bf16[576,1152]{1,0:T(8,128)(2,1)} %param.20), kind=kOutput, calls=%fused_computation.16 | convolution fusion | flops 511377408 | bytes 4423680 | tf_op jit(solution)/shard_map/dot_general | solution.py:134
  (18 shorter events, 0.2 us)
Async XLA Ops:
  0.0 28.8 %copy-start = (bf16[576,1152]{1,0:T(8,128)(2,1)S(1)}, bf16[576,1152]{1,0:T(8,128)(2,1)}, u32[]{:S(2)}) copy-start(bf16[576,1152]{1,0:T(8,128)(2,1)} %param.18) | copy-start | bytes 3981316
  0.0 11.9 %copy-start.1 = (bf16[1,384,1152]{2,1,0:T(8,128)(2,1)S(1)}, bf16[1,384,1152]{2,1,0:T(8,128)(2,1)}, u32[]{:S(2)}) copy-start(bf16[1,384,1152]{2,1,0:T(8,128)(2,1)} %param.11) | copy-start | bytes 2654212
  0.0 11.9 %copy-start.7 = (f32[1152]{0:T(1024)S(1)}, f32[1152]{0:T(1024)}, u32[]{:S(2)}) copy-start(f32[1152]{0:T(1024)} %param.15) | copy-start | bytes 13828
  1.6 30.2 %all-to-all-start.1 = ((bf16[16,1,24]{2,1,0:T(2,128)(2,1)}), bf16[16,1,24]{2,1,0:T(2,128)(2,1)S(1)}, u32[]{:S(2)}, u32[]{:S(2)}) async-start(bf16[16,1,24]{2,1,0:T(2,128)(2,1)} %copy.62), calls=%async_computation.1 | async-start | bytes 16384 | tf_op jit(solution)/shard_map/all_to_all | solution.py:129
  16.8 1.5 %copy-start.3 = (f32[384,3,8,72]{0,3,2,1:T(8,128)}, f32[384,3,8,72]{0,3,2,1:T(8,128)S(1)}, u32[]{:S(2)}) copy-start(f32[384,3,8,72]{0,3,2,1:T(8,128)S(1)} %fusion.26) | copy-start | bytes 7962628
  18.3 0.7 copy-start.8
  18.3 1.8 %copy-start.6 = (f32[4,72]{1,0:T(4,128)S(1)}, f32[4,72]{1,0:T(4,128)}, u32[]{:S(2)}) copy-start(f32[4,72]{1,0:T(4,128)} %param.21) | copy-start | bytes 3460
  25.5 3.2 %copy-start.2 = (bf16[1,384,1152]{2,1,0:T(8,128)(2,1)S(1)}, bf16[1,384,1152]{2,1,0:T(8,128)(2,1)}, u32[]{:S(2)}) copy-start(bf16[1,384,1152]{2,1,0:T(8,128)(2,1)} %param.11) | copy-start | bytes 2654212
  29.9 0.7 copy-start.4
  30.6 7.3 %copy-start.5 = (s32[8,8]{1,0:T(8,128)S(1)}, s32[8,8]{1,0:T(8,128)}, u32[]{:S(2)}) copy-start(s32[8,8]{1,0:T(8,128)} %param.14) | copy-start | bytes 772
  31.8 26.4 %all-to-all-start = ((bf16[16,24,1152]{2,1,0:T(8,128)(2,1)}), bf16[16,24,1152]{2,1,0:T(8,128)(2,1)}, u32[]{:S(2)}, u32[]{:S(2)}) async-start(bf16[16,24,1152]{2,1,0:T(8,128)(2,1)} %bitcast.89), calls=%async_computation | async-start | bytes 1769472 | tf_op jit(solution)/shard_map/all_to_all | solution.py:117
where the time goes:
time: 104 us
  matrix products  29.9 us (29%)
  blocking collectives  19.8 us (19%)
  waiting for transfers between devices  19.3 us (19%)
  starting transfers between devices  13.4 us (13%)
  local copies, waits for them, and re-layouts  13.3 us (13%)
  other arithmetic  7.71 us (7%)
    all_to_all x1, blocking collectives, body(): lax.all_to_all(attended, 'tm', split_axis=0, concat_axis=0, tiled=True)  19.8 us
    all_to_all x1, waiting for transfers between devices, body(): lax.all_to_all(normed.reshape(members, per_peer, model_width), 'tm', spli...  19.3 us
    dot_general x2, matrix products, qkv_heads(): jnp.dot(normed.reshape(-1, normed.shape[-1]), matrix, preferred_element_t...  9.76 us
    sub x2, matrix products, softmax_rows(): exponent = jnp.exp(scores - highest)  9.5 us
    all_to_all x1, starting transfers between devices, body(): lax.all_to_all(usable_marks, 'tm', split_axis=0, concat_axis=0, tiled=True)  7.37 us
    all_to_all x1, starting transfers between devices, body(): lax.all_to_all(normed.reshape(members, per_peer, model_width), 'tm', spli...  6.07 us
    another operation x2, local copies, waits for them, and re-layouts  4.68 us
    dot_general x1, matrix products, spatial_frame(): jnp.einsum('hqk,khd->qhd', weights, packed[:, 2], preferred_element_type=...  3.22 us
  transfers between devices with their start and end apart: 2, of which 1 were waited for; matrix products, arithmetic and copies ran while one was open for 20% of the time, Pallas kernels for 0%

commit v1 on v0

v1 whole, which is shorter than its diff:
```python
import functools

import jax
import jax.numpy as jnp
from jax import lax
from jax.experimental import pallas as pl
from jax.experimental.pallas import tpu as pltpu
from jax.sharding import PartitionSpec as P

HEADS = 8
HD = 72
CAMS = 6
NBLK = 8
UNIT = 16
ROWS = 128
LANES = 128
EPS = 1e-06
SCALE = HD ** (-0.5)
NEG = -1e30
F32, BF16, I32 = jnp.float32, jnp.bfloat16, jnp.int32


def normalize(values, gain):
    average = jnp.mean(values, -1, keepdims=True)
    centred = values - average
    spread = jnp.mean(centred * centred, -1, keepdims=True)
    return (centred * lax.rsqrt(spread + EPS) * gain).astype(BF16)


def split_sum(values, table):
    high = values.astype(BF16)
    low = (values - high.astype(F32)).astype(BF16)
    return jnp.dot(high, table, preferred_element_type=F32) + jnp.dot(
        low, table, preferred_element_type=F32
    )


def project(rows, weight, gain, sums, spreads, q_ref, k_ref, v_ref, at):
    width = HEADS * HD
    packed = jnp.dot(rows, weight[...], preferred_element_type=F32)
    qk = packed[:, : 2 * width]
    total = split_sum(qk * qk, sums[...])
    inverse = lax.rsqrt(total * (1.0 / HD) + EPS)
    high = inverse.astype(BF16).astype(F32)
    lane = lax.broadcasted_iota(I32, inverse.shape, 1)
    both = jnp.where(lane < 2 * HEADS, high, inverse - high).astype(BF16)
    spread = jnp.dot(both, spreads[...], preferred_element_type=F32)
    normed = (qk * spread * gain).astype(BF16)
    q_ref[at, :width] = normed[:, :width]
    k_ref[at, :width] = normed[:, width:]
    v_ref[at, :width] = packed[:, 2 * width :].astype(BF16)


def attend(q_ref, k_ref, v_ref, q_at, k_at, bias):
    tiles = [None] * (-(-HEADS * HD // LANES))
    for head in range(HEADS):
        first, last = head * HD // LANES, ((head + 1) * HD - 1) // LANES
        window = slice(first * LANES, (last + 1) * LANES)
        lane = lax.broadcasted_iota(I32, (1, (last + 1 - first) * LANES), 1) + first * LANES
        inside = (lane >= head * HD) & (lane < (head + 1) * HD)
        queries = q_ref[q_at, window] * jnp.where(inside, 1.0, 0.0).astype(BF16)
        scores = lax.dot_general(
            queries, k_ref[k_at, window], (((1,), (1,)), ((), ())), preferred_element_type=F32
        )
        scores = scores * SCALE + bias
        exponent = jnp.exp(scores - jnp.max(scores, -1, keepdims=True))
        weights = exponent * (1.0 / jnp.sum(exponent, -1, keepdims=True))
        part = jnp.dot(weights.astype(BF16), v_ref[k_at, window], preferred_element_type=F32)
        part = jnp.where(inside, part, 0.0)
        for tile in range(first, last + 1):
            piece = part[:, (tile - first) * LANES : (tile - first + 1) * LANES]
            tiles[tile] = piece if tiles[tile] is None else tiles[tile] + piece
    return jnp.concatenate(tiles, 1).astype(BF16)


def kernel(
    n,
    cam_len,
    view_mask,
    time_mask,
    video,
    cam_row,
    s_gain,
    t_gain,
    s_qk,
    t_qk,
    s_qkv_hbm,
    s_out_hbm,
    t_qkv_hbm,
    t_out_hbm,
    out,
    s_qkv,
    s_out,
    t_qkv,
    t_out,
    sums,
    spreads,
    sq,
    sk,
    sv,
    tq,
    tk,
    tv,
    after,
    sending,
    received,
    attended,
    returned,
    cams_all,
    links,
    weight_sem,
    cam_send,
    cam_recv,
    go_send,
    go_recv,
    back_send,
    back_recv,
):
    slots, model = after.shape
    width = HEADS * HD
    third = slots // (3 * UNIT)
    stride = (n // 2) // third
    me = lax.axis_index("tm")
    my_chip, my_core = me // 2, me % 2
    my_item = my_chip // stride
    working = (my_chip % stride) == 0
    my_units = jnp.where(working, 2 - my_core, 0)
    other = lax.rem(me + 1, n)

    loads = [
        pltpu.make_async_copy(src, dst, weight_sem.at[i])
        for i, (src, dst) in enumerate(
            ((s_qkv_hbm, s_qkv), (s_out_hbm, s_out), (t_qkv_hbm, t_qkv), (t_out_hbm, t_out))
        )
    ]
    for load in loads:
        load.start()

    barrier = pltpu.get_barrier_semaphore()

    def greet(step, carry):
        peer = lax.rem(me + step, n)
        pl.semaphore_signal(
            barrier, inc=1, device_id={"tm": peer}, device_id_type=pl.DeviceIdType.MESH
        )
        return carry

    lax.fori_loop(1, n, greet, 0)

    entry = lax.broadcasted_iota(I32, sums.shape, 0)
    head = lax.broadcasted_iota(I32, sums.shape, 1)
    head = jnp.where(head < 2 * HEADS, head, head - 2 * HEADS) * HD
    sums[...] = jnp.where((entry >= head) & (entry < head + HD), 1.0, 0.0).astype(BF16)
    entry = lax.broadcasted_iota(I32, spreads.shape, 1)
    head = lax.broadcasted_iota(I32, spreads.shape, 0)
    head = jnp.where(head < 2 * HEADS, head, head - 2 * HEADS) * HD
    spreads[...] = jnp.where((entry >= head) & (entry < head + HD), 1.0, 0.0).astype(BF16)
    for ref in (sq, sk, sv, tq, tk, tv):
        ref[:, width:] = jnp.zeros((ref.shape[0], ref.shape[1] - width), BF16)

    def to_normed(step, carry):
        at = pl.ds(pl.multiple_of(step * 64, 64), 64)
        sending[at, :] = normalize(video[0, at, :].astype(F32), s_gain[...])
        return carry

    lax.fori_loop(0, slots // 64, to_normed, 0)
    loads[0].wait()

    def to_heads(step, carry):
        at = pl.ds(pl.multiple_of(step * ROWS, ROWS), ROWS)
        project(sending[at, :], s_qkv, s_qk[...], sums, spreads, sq, sk, sv, at)
        return carry

    lax.fori_loop(0, slots // ROWS, to_heads, 0)

    pl.semaphore_wait(barrier, n - 1)

    def device_of(item, core):
        return item * (2 * stride) + core

    def cam_copy(item, core, frame):
        return pltpu.make_async_remote_copy(
            src_ref=cam_row,
            dst_ref=cams_all.at[frame],
            send_sem=cam_send.at[core, item],
            recv_sem=cam_recv.at[frame],
            device_id={"tm": device_of(item, core)},
            device_id_type=pl.DeviceIdType.MESH,
        )

    for core in range(2):

        def send_cams(item, carry):
            @pl.when(device_of(item, core) != me)
            def _():
                cam_copy(item, core, me).start()

            return carry

        lax.fori_loop(0, third, send_cams, 0)

    def go_copy(part, item, frame):
        core, slot = (1, 0) if part == 1 else (0, part // 2)
        at = pl.ds(pl.multiple_of((part * third + item) * UNIT, UNIT), UNIT)
        return pltpu.make_async_remote_copy(
            src_ref=sending.at[at],
            dst_ref=received.at[slot, pl.ds(pl.multiple_of(frame * UNIT, UNIT), UNIT)],
            send_sem=go_send.at[part, item],
            recv_sem=go_recv.at[slot, frame],
            device_id={"tm": device_of(item, core)},
            device_id_type=pl.DeviceIdType.MESH,
        )

    camera = lax.broadcasted_iota(I32, (1, slots), 1)
    tile = slots // CAMS
    length = jnp.zeros((1, slots), I32)
    for cam in range(CAMS):
        length = jnp.where(
            (camera >= cam * tile) & (camera < (cam + 1) * tile), cam_len[0, cam] + cam * tile, length
        )
    live = camera < length

    def camera_bias(query):
        seen = jnp.zeros((1, slots), I32)
        for cam in range(CAMS):
            mark = jnp.int32(1) if cam == query else view_mask[query, cam]
            seen = jnp.where((camera >= cam * tile) & (camera < (cam + 1) * tile), mark, seen)
        row = jnp.where((seen > 0) & live, 0.0, NEG)
        return jnp.broadcast_to(row, (tile, slots))

    loads[1].wait()
    per = ROWS // tile
    for part in range(3):
        at = pl.ds(part * ROWS, ROWS)
        bias = jnp.concatenate([camera_bias(part * per + i) for i in range(per)], 0)
        heads = attend(sq, sk, sv, at, slice(None), bias)[:, :width]
        mixed = jnp.dot(heads, s_out[...], preferred_element_type=F32)
        after_space = (video[0, at, :].astype(F32) + mixed).astype(BF16)
        after[at, :] = after_space
        sending[at, :] = normalize(after_space.astype(F32), t_gain[...])
        core, slot = (1, 0) if part == 1 else (0, part // 2)

        def send_part(step, carry):
            item = lax.rem(my_item + step, third)

            @pl.when(device_of(item, core) != me)
            def _():
                go_copy(part, item, me).start()

            return carry

        lax.fori_loop(0, third, send_part, 0)

        @pl.when(working & (my_core == core))
        def _():
            own = pl.ds(pl.multiple_of((part * third + my_item) * UNIT, UNIT), UNIT)
            received[slot, pl.ds(pl.multiple_of(me * UNIT, UNIT), UNIT), :] = sending[own, :]

    loads[2].wait()

    @pl.when(working)
    def _():
        cams_all[me] = cam_row[...]

        def cam_arrived(step, carry):
            cam_copy(0, 0, lax.rem(me + step, n)).wait_recv()
            return carry

        lax.fori_loop(1, n, cam_arrived, 0)

    span = n * UNIT
    block = span // NBLK

    def unit_of(slot):
        part = jnp.where(my_core == 1, 1, 2 * slot)
        return part * third + my_item

    def back_copy(slot, frame, unit):
        return pltpu.make_async_remote_copy(
            src_ref=attended.at[slot, pl.ds(pl.multiple_of(frame * UNIT, UNIT), UNIT)],
            dst_ref=returned.at[pl.ds(pl.multiple_of(unit * UNIT, UNIT), UNIT)],
            send_sem=back_send.at[slot, frame],
            recv_sem=back_recv.at[unit],
            device_id={"tm": frame},
            device_id_type=pl.DeviceIdType.MESH,
        )

    def work(slot, carry):
        unit = unit_of(slot)

        def arrived(step, inner):
            frame = lax.rem(me + step, n)
            pltpu.make_async_remote_copy(
                src_ref=sending.at[pl.ds(0, UNIT)],
                dst_ref=received.at[slot, pl.ds(pl.multiple_of(frame * UNIT, UNIT), UNIT)],
                send_sem=go_send.at[0, 0],
                recv_sem=go_recv.at[slot, frame],
                device_id={"tm": other},
                device_id_type=pl.DeviceIdType.MESH,
            ).wait_recv()
            return inner

        lax.fori_loop(1, n, arrived, 0)

        def heads_of(step, inner):
            at = pl.ds(pl.multiple_of(step * ROWS, ROWS), ROWS)
            project(received[slot, at, :], t_qkv, t_qk[...], sums, spreads, tq, tk, tv, at)
            return inner

        lax.fori_loop(0, span // ROWS, heads_of, 0)

        per_camera = tile // UNIT
        cam_lane = lax.broadcasted_iota(I32, (n, LANES), 1)
        cam_col = jnp.sum(
            jnp.where(cam_lane == unit // per_camera, cams_all[:, 0, :], 0), 1, keepdims=True
        )
        key = lax.broadcasted_iota(I32, (n, span), 1)
        begin = lax.broadcasted_iota(I32, (n, span), 0) * UNIT
        mine = (key >= begin) & (key < begin + UNIT)
        spot = key - begin + lax.rem(unit, per_camera) * UNIT
        usable = jnp.sum(jnp.where(mine & (spot < cam_col), 1.0, 0.0), 0, keepdims=True)
        column = lax.broadcasted_iota(I32, (1, span), 1)
        for query in range(NBLK):
            marks = jnp.zeros((1, span), I32)
            for other_block in range(NBLK):
                inside = (column >= other_block * block) & (column < (other_block + 1) * block)
                marks = jnp.where(inside, time_mask[query, other_block], marks)
            links[query : query + 1, :] = jnp.where(marks > 0, usable, 0.0)

        def mix(step, inner):
            at = pl.ds(pl.multiple_of(step * ROWS, ROWS), ROWS)
            row = lax.broadcasted_iota(I32, (ROWS, 1), 0) + step * ROWS
            mark = jnp.zeros((ROWS, span), F32)
            for query in range(NBLK):
                inside = (row >= query * block) & (row < (query + 1) * block)
                mark = jnp.where(inside, links[query : query + 1, :], mark)
            row_frame, column_frame = row // UNIT, column // UNIT
            same_slot = (row - row_frame * UNIT) == (column - column_frame * UNIT)
            earlier = (row_frame > column_frame) & (mark > 0.5)
            bias = jnp.where(same_slot & ((row_frame == column_frame) | earlier), 0.0, NEG)
            attended[slot, at, :] = attend(tq, tk, tv, at, slice(None), bias)[:, :width]
            return inner

        lax.fori_loop(0, span // ROWS, mix, 0)

        def send_back(step, inner):
            back_copy(slot, lax.rem(me + step, n), unit).start()
            return inner

        lax.fori_loop(1, n, send_back, 0)
        own = pl.ds(pl.multiple_of(me * UNIT, UNIT), UNIT)
        returned[pl.ds(pl.multiple_of(unit * UNIT, UNIT), UNIT), :] = attended[slot, own, :]
        return carry

    lax.fori_loop(0, my_units, work, 0)

    loads[3].wait()
    for part in range(3):
        core = 1 if part == 1 else 0

        def came_back(item, carry):
            @pl.when(device_of(item, core) != me)
            def _():
                unit = part * third + item
                pltpu.make_async_remote_copy(
                    src_ref=attended.at[0, pl.ds(0, UNIT)],
                    dst_ref=returned.at[pl.ds(pl.multiple_of(unit * UNIT, UNIT), UNIT)],
                    send_sem=back_send.at[0, 0],
                    recv_sem=back_recv.at[unit],
                    device_id={"tm": other},
                    device_id_type=pl.DeviceIdType.MESH,
                ).wait_recv()

            return carry

        lax.fori_loop(0, third, came_back, 0)
        at = pl.ds(part * ROWS, ROWS)
        mixed = jnp.dot(returned[at, :], t_out[...], preferred_element_type=F32).astype(BF16)
        out[0, at, :] = (after[at, :].astype(F32) + mixed.astype(F32)).astype(BF16)

    for core in range(2):

        def cams_sent(item, carry):
            @pl.when(device_of(item, core) != me)
            def _():
                cam_copy(item, core, me).wait_send()

            return carry

        lax.fori_loop(0, third, cams_sent, 0)
    for part in range(3):
        core = 1 if part == 1 else 0

        def part_sent(item, carry):
            @pl.when(device_of(item, core) != me)
            def _():
                go_copy(part, item, me).wait_send()

            return carry

        lax.fori_loop(0, third, part_sent, 0)

    def unit_sent(slot, carry):
        def frame_sent(step, inner):
            back_copy(slot, lax.rem(me + step, n), unit_of(slot)).wait_send()
            return inner

        return lax.fori_loop(1, n, frame_sent, carry)

    lax.fori_loop(0, my_units, unit_sent, 0)


def body(
    n, video, cam_len, view_mask, time_mask, s_gain, t_gain, s_qkv, s_out, t_qkv, t_out, qk_gain
):
    _, slots, model = video.shape
    width = HEADS * HD
    padded = -(-width // LANES) * LANES
    span = n * UNIT
    third = slots // (3 * UNIT)
    cam_row = jnp.broadcast_to(
        jnp.pad(cam_len, ((0, 0), (0, LANES - cam_len.shape[1]))), (8, LANES)
    )
    gains = jnp.broadcast_to(qk_gain[:, None, :], (4, HEADS, HD)).reshape(2, 1, 2 * width)
    smem = pl.BlockSpec(memory_space=pltpu.SMEM)
    vmem = pl.BlockSpec(memory_space=pltpu.VMEM)
    hbm = pl.BlockSpec(memory_space=pl.ANY)
    dma = pltpu.SemaphoreType.DMA
    return pl.pallas_call(
        functools.partial(kernel, n),
        out_shape=jax.ShapeDtypeStruct(video.shape, BF16),
        in_specs=[smem] * 3 + [vmem] * 6 + [hbm] * 4,
        out_specs=vmem,
        scratch_shapes=[
            pltpu.VMEM(s_qkv.shape, BF16),
            pltpu.VMEM(s_out.shape, BF16),
            pltpu.VMEM(t_qkv.shape, BF16),
            pltpu.VMEM(t_out.shape, BF16),
            pltpu.VMEM((2 * width, LANES), BF16),
            pltpu.VMEM((LANES, 2 * width), BF16),
            *[pltpu.VMEM((slots, padded), BF16)] * 3,
            *[pltpu.VMEM((span, padded), BF16)] * 3,
            pltpu.VMEM((slots, model), BF16),
            pltpu.VMEM((slots, model), BF16),
            pltpu.VMEM((2, span, model), BF16),
            pltpu.VMEM((2, span, width), BF16),
            pltpu.VMEM((slots, width), BF16),
            pltpu.VMEM((n, 8, LANES), I32),
            pltpu.VMEM((NBLK, span), F32),
            dma((4,)),
            dma((2, third)),
            dma((n,)),
            dma((3, third)),
            dma((2, n)),
            dma((2, n)),
            dma((3 * third,)),
        ],
        compiler_params=pltpu.CompilerParams(
            collective_id=0, has_side_effects=True, vmem_limit_bytes=58 * 1024 * 1024
        ),
        cost_estimate=pl.CostEstimate(
            flops=6_000_000_000, bytes_accessed=13_000_000, transcendentals=2_400_000
        ),
    )(
        cam_len,
        view_mask,
        time_mask,
        video,
        cam_row,
        s_gain[None],
        t_gain[None],
        gains[0],
        gains[1],
        s_qkv,
        s_out,
        t_qkv,
        t_out,
    )


def solution(mesh):
    placed = (P(("groups", "tm"), None, None), P(("groups", "tm"), None)) + (P(),) * 9
    return jax.shard_map(
        functools.partial(body, mesh.shape["tm"]),
        mesh=mesh,
        in_specs=placed,
        out_specs=P(("groups", "tm"), None, None),
        check_vma=False,
    )
```

time: 104 us -> 71.5 us (0.69)
  Pallas kernels: 0 us -> 50 us
  matrix products: 29.9 us -> 0 us
  blocking collectives: 19.8 us -> 0 us
  waiting for transfers between devices: 19.3 us -> 0 us
  starting transfers between devices: 13.4 us -> 0 us
  other arithmetic: 7.71 us -> 0 us
  local copies, waits for them, and re-layouts: 13.3 us -> 21 us
    pallas_call x0 -> x1, Pallas kernels: none -> 50 us  [body(): pl.pallas_call(functools.partial(kernel, n), out_shape=jax.ShapeDtypeStru...]
    dot_general x8 -> x0, matrix products: 20.4 us -> none  [the longest x2 9.76 us: qkv_heads(): jnp.dot(normed.reshape(-1, normed.shape[-1]), matrix, preferred_element_t...]
    all_to_all x1 -> x0, blocking collectives: 19.8 us -> none  [body(): lax.all_to_all(attended, 'tm', split_axis=0, concat_axis=0, tiled=True)]
    all_to_all x2 -> x0, waiting for transfers between devices: 19.3 us -> none  [the longest x1 19.3 us: body(): lax.all_to_all(normed.reshape(members, per_peer, model_width), 'tm', spli...]
    all_to_all x2 -> x0, starting transfers between devices: 13.4 us -> none  [the longest x1 7.37 us: body(): lax.all_to_all(usable_marks, 'tm', split_axis=0, concat_axis=0, tiled=True)]
    unnamed x18 -> x3, local copies, waits for them, and re-layouts: 2.44 us -> 15 us
    sub x2 -> x0, matrix products: 9.5 us -> none  [softmax_rows(): exponent = jnp.exp(scores - highest)]
    another operation x2 -> x0, local copies, waits for them, and re-layouts: 4.68 us -> none
  transfers between devices with their start and end apart: 2 -> 0, of which waited for: 1 -> 0; matrix products, arithmetic and copies ran while one was open for 20% -> 0% of each run, Pallas kernels for 0% -> 0%
where the time goes in v1:
time: 71.5 us; the launch traced here: 70.9 us
  Pallas kernels  50 us (70%)
  local copies, waits for them, and re-layouts  21 us (29%)
    pallas_call x1, Pallas kernels, body(): pl.pallas_call(functools.partial(kernel, n), out_shape=jax.ShapeDtypeStru...  50 us
    unnamed x3, local copies, waits for them, and re-layouts  15 us

profile of v1, /device:TPU:0, one launch (start us, length us, event | category | flops | bytes accessed | tf_op | source)
XLA Modules:
  0.0 70.9 jit_solution(1988885570098697760)
XLA Ops:
  0.0 0.7 pad_bitcast_fusion
  0.7 0.8 %fusion = (f32[2,72]{1,0:T(2,128)S(1)}, f32[2,72]{1,0:T(2,128)S(1)}) fusion(f32[4,72]{1,0:T(4,128)} %param.21), kind=kLoop, calls=%fused_computation.1 | loop fusion | bytes 2304 | tf_op jit(solution)/shard_map/slice | solution.py:473
  1.4 0.6 broadcast_in_dim.22.cam_row
  2.0 1.3 %broadcast_in_dim.23.s_gain = f32[1,1152]{1,0:T(1,128)} reshape(f32[1152]{0:T(1024)} %param.15) | data formatting | bytes 9216 | tf_op jit(solution)/shard_map/broadcast_in_dim | solution.py:470
  3.3 1.3 %broadcast_in_dim.24.t_gain = f32[1,1152]{1,0:T(1,128)} reshape(f32[1152]{0:T(1024)} %param.16) | data formatting | bytes 9216 | tf_op jit(solution)/shard_map/broadcast_in_dim | solution.py:471
  4.6 0.7 squeeze.7.t_qk
  5.3 0.7 squeeze.6.s_qk
  6.0 6.4 %copy.12.s_qkv_hbm = bf16[1152,1728]{1,0:T(8,128)(2,1)} copy(bf16[1152,1728]{0,1:T(8,128)(2,1)} %param.17) | data formatting | bytes 7962624 | tf_op args[6]
  12.4 6.4 %copy.13.t_qkv_hbm = bf16[1152,1728]{1,0:T(8,128)(2,1)} copy(bf16[1152,1728]{0,1:T(8,128)(2,1)} %param.19) | data formatting | bytes 7962624 | tf_op args[8]
  18.8 50.0 %shard_map.109 = bf16[1,384,1152]{2,1,0:T(8,128)(2,1)} custom-call(s32[1,6]{1,0:T(1,128)} %cam_len.1, s32[6,6]{1,0:T(8,128)} %view_mask.1, s32[8,8]{1,0:T(8,128)} %time_mask.1, bf16[1,384,1152]{2,1,0:T(8,128)(2,1)} %video.1, s32[8,128]{1,0:T(8,128)} %broadcast_in_dim.22.cam_row, f32[1,1152]{1,0:T(1,128)} %broadcast_in_dim.23.s_gain, ...), custom_call_target="tpu_custom_call" | custom-call | flops 6000000000 | bytes 13000000 | tf_op jit(solution)/shard_map/pallas_call | solution.py:429
  68.8 2.1 %copy.15 = bf16[1,384,1152]{2,1,0:T(8,128)(2,1)} copy(bf16[1,384,1152]{2,1,0:T(8,128)(2,1)} %shard_map.109) | data formatting | bytes 1769472
  (2 shorter events, 0.0 us)

commit v2 on v1

--- a/solution.py
+++ b/solution.py
@@ -37,7 +37,9 @@
 
 def project(rows, weight, gain, sums, spreads, q_ref, k_ref, v_ref, at):
     width = HEADS * HD
-    packed = jnp.dot(rows, weight[...], preferred_element_type=F32)
+    packed = lax.dot_general(
+        rows, weight[...], (((1,), (1,)), ((), ())), preferred_element_type=F32
+    )
     qk = packed[:, : 2 * width]
     total = split_sum(qk * qk, sums[...])
     inverse = lax.rsqrt(total * (1.0 / HD) + EPS)
@@ -79,11 +81,9 @@
     view_mask,
     time_mask,
     video,
-    cam_row,
     s_gain,
     t_gain,
-    s_qk,
-    t_qk,
+    qk_gain,
     s_qkv_hbm,
     s_out_hbm,
     t_qkv_hbm,
@@ -106,6 +106,7 @@
     received,
     attended,
     returned,
+    cam_row,
     cams_all,
     links,
     weight_sem,
@@ -155,23 +156,27 @@
     head = lax.broadcasted_iota(I32, spreads.shape, 0)
     head = jnp.where(head < 2 * HEADS, head, head - 2 * HEADS) * HD
     spreads[...] = jnp.where((entry >= head) & (entry < head + HD), 1.0, 0.0).astype(BF16)
+    lane = lax.broadcasted_iota(I32, cam_row.shape, 1)
+    lengths = jnp.zeros(cam_row.shape, I32)
+    for cam in range(CAMS):
+        lengths = jnp.where(lane == cam, cam_len[0, cam], lengths)
+    cam_row[...] = lengths
     for ref in (sq, sk, sv, tq, tk, tv):
         ref[:, width:] = jnp.zeros((ref.shape[0], ref.shape[1] - width), BF16)
 
+    def qk_row(first):
+        pair = [qk_gain[first + i : first + i + 1, :] for i in range(2)]
+        return jnp.concatenate([pair[0]] * HEADS + [pair[1]] * HEADS, 1)
+
     def to_normed(step, carry):
         at = pl.ds(pl.multiple_of(step * 64, 64), 64)
-        sending[at, :] = normalize(video[0, at, :].astype(F32), s_gain[...])
+        sending[at, :] = normalize(video[0, at, :].astype(F32), s_gain[...][None, :])
         return carry
 
     lax.fori_loop(0, slots // 64, to_normed, 0)
     loads[0].wait()
 
-    def to_heads(step, carry):
-        at = pl.ds(pl.multiple_of(step * ROWS, ROWS), ROWS)
-        project(sending[at, :], s_qkv, s_qk[...], sums, spreads, sq, sk, sv, at)
-        return carry
-
-    lax.fori_loop(0, slots // ROWS, to_heads, 0)
+    project(sending[...], s_qkv, qk_row(0), sums, spreads, sq, sk, sv, slice(None))
 
     pl.semaphore_wait(barrier, n - 1)
 
@@ -237,7 +242,7 @@
         mixed = jnp.dot(heads, s_out[...], preferred_element_type=F32)
         after_space = (video[0, at, :].astype(F32) + mixed).astype(BF16)
         after[at, :] = after_space
-        sending[at, :] = normalize(after_space.astype(F32), t_gain[...])
+        sending[at, :] = normalize(after_space.astype(F32), t_gain[...][None, :])
         core, slot = (1, 0) if part == 1 else (0, part // 2)
 
         def send_part(step, carry):
@@ -303,11 +308,11 @@
         lax.fori_loop(1, n, arrived, 0)
 
         def heads_of(step, inner):
-            at = pl.ds(pl.multiple_of(step * ROWS, ROWS), ROWS)
-            project(received[slot, at, :], t_qkv, t_qk[...], sums, spreads, tq, tk, tv, at)
+            at = pl.ds(pl.multiple_of(step * 2 * ROWS, ROWS), 2 * ROWS)
+            project(received[slot, at, :], t_qkv, qk_row(2), sums, spreads, tq, tk, tv, at)
             return inner
 
-        lax.fori_loop(0, span // ROWS, heads_of, 0)
+        lax.fori_loop(0, span // (2 * ROWS), heads_of, 0)
 
         per_camera = tile // UNIT
         cam_lane = lax.broadcasted_iota(I32, (n, LANES), 1)
@@ -418,10 +423,6 @@
     padded = -(-width // LANES) * LANES
     span = n * UNIT
     third = slots // (3 * UNIT)
-    cam_row = jnp.broadcast_to(
-        jnp.pad(cam_len, ((0, 0), (0, LANES - cam_len.shape[1]))), (8, LANES)
-    )
-    gains = jnp.broadcast_to(qk_gain[:, None, :], (4, HEADS, HD)).reshape(2, 1, 2 * width)
     smem = pl.BlockSpec(memory_space=pltpu.SMEM)
     vmem = pl.BlockSpec(memory_space=pltpu.VMEM)
     hbm = pl.BlockSpec(memory_space=pl.ANY)
@@ -429,12 +430,12 @@
     return pl.pallas_call(
         functools.partial(kernel, n),
         out_shape=jax.ShapeDtypeStruct(video.shape, BF16),
-        in_specs=[smem] * 3 + [vmem] * 6 + [hbm] * 4,
+        in_specs=[smem] * 3 + [vmem] * 4 + [hbm] * 4,
         out_specs=vmem,
         scratch_shapes=[
-            pltpu.VMEM(s_qkv.shape, BF16),
+            pltpu.VMEM(s_qkv.shape[::-1], BF16),
             pltpu.VMEM(s_out.shape, BF16),
-            pltpu.VMEM(t_qkv.shape, BF16),
+            pltpu.VMEM(t_qkv.shape[::-1], BF16),
             pltpu.VMEM(t_out.shape, BF16),
             pltpu.VMEM((2 * width, LANES), BF16),
             pltpu.VMEM((LANES, 2 * width), BF16),
@@ -445,6 +446,7 @@
             pltpu.VMEM((2, span, model), BF16),
             pltpu.VMEM((2, span, width), BF16),
             pltpu.VMEM((slots, width), BF16),
+            pltpu.VMEM((8, LANES), I32),
             pltpu.VMEM((n, 8, LANES), I32),
             pltpu.VMEM((NBLK, span), F32),
             dma((4,)),
@@ -466,14 +468,12 @@
         view_mask,
         time_mask,
         video,
-        cam_row,
-        s_gain[None],
-        t_gain[None],
-        gains[0],
-        gains[1],
-        s_qkv,
+        s_gain,
+        t_gain,
+        qk_gain,
+        s_qkv.T,
         s_out,
-        t_qkv,
+        t_qkv.T,
         t_out,
     )
 

time: 71.5 us -> 51.3 us (0.72)
  local copies, waits for them, and re-layouts: 21 us -> 2.15 us
  Pallas kernels: 50 us -> 49 us
    unnamed x3 -> x1, local copies, waits for them, and re-layouts: 15 us -> 2.15 us
    broadcast_in_dim x6 -> x0, local copies, waits for them, and re-layouts: 3.83 us -> none  [the longest x1 1.29 us: body(): s_gain[None]]
    squeeze x2 -> x0, local copies, waits for them, and re-layouts: 1.37 us -> none  [the longest x1 0.69 us: body(): gains[0]]
    pallas_call x1, Pallas kernels: 50 us -> 49 us  [body(): pl.pallas_call(functools.partial(kernel, n), out_shape=jax.ShapeDtypeStru...]
    slice x1 -> x0, local copies, waits for them, and re-layouts: 0.76 us -> none  [body(): gains[1]]
where the time goes in v2:
time: 51.3 us; the launch traced here: 51.1 us
  Pallas kernels  49 us (96%)
  local copies, waits for them, and re-layouts  2.15 us (4%)
    pallas_call x1, Pallas kernels, body(): pl.pallas_call(functools.partial(kernel, n), out_shape=jax.ShapeDtypeStru...  49 us
    unnamed x1, local copies, waits for them, and re-layouts  2.15 us

profile of v2, /device:TPU:0, one launch (start us, length us, event | category | flops | bytes accessed | tf_op | source)
XLA Modules:
  0.0 51.1 jit_solution(12712633543471070118)
XLA Ops:
  0.0 49.0 %shard_map.109 = bf16[1,384,1152]{2,1,0:T(8,128)(2,1)} custom-call(s32[1,6]{1,0:T(1,128)} %cam_len.1, s32[6,6]{1,0:T(8,128)} %view_mask.1, s32[8,8]{1,0:T(8,128)} %time_mask.1, bf16[1,384,1152]{2,1,0:T(8,128)(2,1)} %video.1, f32[1152]{0:T(1024)} %s_gain.1, f32[1152]{0:T(1024)} %t_gain.1, f32[4,72]{1,0:T(4,128)} %qk_gain.1, bf16[1728,1152]{1,0:T(8,128)(2,1)} %bitcast.2, ...), custom_call_target="tpu_custom_call" | custom-call | flops 6000000000 | bytes 13000000 | tf_op jit(solution)/shard_map/pallas_call | solution.py:430
  49.0 2.1 %copy.13 = bf16[1,384,1152]{2,1,0:T(8,128)(2,1)} copy(bf16[1,384,1152]{2,1,0:T(8,128)(2,1)} %shard_map.109) | data formatting | bytes 1769472

commit v3 on v2

--- a/solution.py
+++ b/solution.py
@@ -55,23 +55,38 @@
 
 def attend(q_ref, k_ref, v_ref, q_at, k_at, bias):
     tiles = [None] * (-(-HEADS * HD // LANES))
-    for head in range(HEADS):
-        first, last = head * HD // LANES, ((head + 1) * HD - 1) // LANES
-        window = slice(first * LANES, (last + 1) * LANES)
-        lane = lax.broadcasted_iota(I32, (1, (last + 1 - first) * LANES), 1) + first * LANES
-        inside = (lane >= head * HD) & (lane < (head + 1) * HD)
-        queries = q_ref[q_at, window] * jnp.where(inside, 1.0, 0.0).astype(BF16)
-        scores = lax.dot_general(
-            queries, k_ref[k_at, window], (((1,), (1,)), ((), ())), preferred_element_type=F32
-        )
-        scores = scores * SCALE + bias
-        exponent = jnp.exp(scores - jnp.max(scores, -1, keepdims=True))
-        weights = exponent * (1.0 / jnp.sum(exponent, -1, keepdims=True))
-        part = jnp.dot(weights.astype(BF16), v_ref[k_at, window], preferred_element_type=F32)
-        part = jnp.where(inside, part, 0.0)
-        for tile in range(first, last + 1):
-            piece = part[:, (tile - first) * LANES : (tile - first + 1) * LANES]
-            tiles[tile] = piece if tiles[tile] is None else tiles[tile] + piece
+    group = HEADS if bias.shape[1] <= 512 else 2
+    for begin in range(0, HEADS, group):
+        views = []
+        for head in range(begin, begin + group):
+            first, last = head * HD // LANES, ((head + 1) * HD - 1) // LANES
+            lane = lax.broadcasted_iota(I32, (1, (last + 1 - first) * LANES), 1) + first * LANES
+            inside = (lane >= head * HD) & (lane < (head + 1) * HD)
+            views.append((first, last, slice(first * LANES, (last + 1) * LANES), inside))
+        scores = []
+        for _, _, window, inside in views:
+            queries = q_ref[q_at, window] * jnp.where(inside, 1.0, 0.0).astype(BF16)
+            scores.append(
+                lax.dot_general(
+                    queries,
+                    k_ref[k_at, window],
+                    (((1,), (1,)), ((), ())),
+                    preferred_element_type=F32,
+                )
+            )
+        weights = []
+        for score in scores:
+            score = score * SCALE + bias
+            exponent = jnp.exp(score - jnp.max(score, -1, keepdims=True))
+            weights.append(
+                (exponent * (1.0 / jnp.sum(exponent, -1, keepdims=True))).astype(BF16)
+            )
+        for weight, (first, last, window, inside) in zip(weights, views):
+            part = jnp.dot(weight, v_ref[k_at, window], preferred_element_type=F32)
+            part = jnp.where(inside, part, 0.0)
+            for tile in range(first, last + 1):
+                piece = part[:, (tile - first) * LANES : (tile - first + 1) * LANES]
+                tiles[tile] = piece if tiles[tile] is None else tiles[tile] + piece
     return jnp.concatenate(tiles, 1).astype(BF16)
 
 
@@ -134,8 +149,7 @@
             ((s_qkv_hbm, s_qkv), (s_out_hbm, s_out), (t_qkv_hbm, t_qkv), (t_out_hbm, t_out))
         )
     ]
-    for load in loads:
-        load.start()
+    loads[0].start()
 
     barrier = pltpu.get_barrier_semaphore()
 
@@ -175,6 +189,8 @@
 
     lax.fori_loop(0, slots // 64, to_normed, 0)
     loads[0].wait()
+    for load in loads[1:]:
+        load.start()
 
     project(sending[...], s_qkv, qk_row(0), sums, spreads, sq, sk, sv, slice(None))
 
@@ -246,7 +262,10 @@
         core, slot = (1, 0) if part == 1 else (0, part // 2)
 
         def send_part(step, carry):
-            item = lax.rem(my_item + step, third)
+            near = third // 2
+            half = my_item // near
+            half = jnp.where(step < near, 1 - half, half)
+            item = half * near + lax.rem(my_item + step, near)
 
             @pl.when(device_of(item, core) != me)
             def _():
@@ -332,9 +351,13 @@
                 marks = jnp.where(inside, time_mask[query, other_block], marks)
             links[query : query + 1, :] = jnp.where(marks > 0, usable, 0.0)
 
+        pieces = span // ROWS
+        far = jnp.where(me < n // 2, pieces // 2, 0)
+
         def mix(step, inner):
-            at = pl.ds(pl.multiple_of(step * ROWS, ROWS), ROWS)
-            row = lax.broadcasted_iota(I32, (ROWS, 1), 0) + step * ROWS
+            piece = lax.rem(step + far, pieces)
+            at = pl.ds(pl.multiple_of(piece * ROWS, ROWS), ROWS)
+            row = lax.broadcasted_iota(I32, (ROWS, 1), 0) + piece * ROWS
             mark = jnp.zeros((ROWS, span), F32)
             for query in range(NBLK):
                 inside = (row >= query * block) & (row < (query + 1) * block)
@@ -344,15 +367,20 @@
             earlier = (row_frame > column_frame) & (mark > 0.5)
             bias = jnp.where(same_slot & ((row_frame == column_frame) | earlier), 0.0, NEG)
             attended[slot, at, :] = attend(tq, tk, tv, at, slice(None), bias)[:, :width]
-            return inner
-
-        lax.fori_loop(0, span // ROWS, mix, 0)
-
-        def send_back(step, inner):
-            back_copy(slot, lax.rem(me + step, n), unit).start()
-            return inner
-
-        lax.fori_loop(1, n, send_back, 0)
+            frames = ROWS // UNIT
+
+            def send_back(turn, deeper):
+                frame = piece * frames + lax.rem(me + turn, frames)
+
+                @pl.when(frame != me)
+                def _():
+                    back_copy(slot, frame, unit).start()
+
+                return deeper
+
+            return lax.fori_loop(0, frames, send_back, inner)
+
+        lax.fori_loop(0, pieces, mix, 0)
         own = pl.ds(pl.multiple_of(me * UNIT, UNIT), UNIT)
         returned[pl.ds(pl.multiple_of(unit * UNIT, UNIT), UNIT), :] = attended[slot, own, :]
         return carry

time: 51.3 us -> 49.3 us (0.961)
  Pallas kernels: 49 us -> 47 us
    pallas_call x1, Pallas kernels: 49 us -> 47 us  [body(): pl.pallas_call(functools.partial(kernel, n), out_shape=jax.ShapeDtypeStru...]
where the time goes in v3:
time: 49.3 us; the launch traced here: 49.1 us
  Pallas kernels  47 us (95%)
  local copies, waits for them, and re-layouts  2.15 us (4%)
    pallas_call x1, Pallas kernels, body(): pl.pallas_call(functools.partial(kernel, n), out_shape=jax.ShapeDtypeStru...  47 us
    unnamed x1, local copies, waits for them, and re-layouts  2.15 us

profile of v3, /device:TPU:0, one launch (start us, length us, event | category | flops | bytes accessed | tf_op | source)
XLA Modules:
  0.0 49.1 jit_solution(14757460216063060478)
XLA Ops:
  0.0 47.0 %shard_map.109 = bf16[1,384,1152]{2,1,0:T(8,128)(2,1)} custom-call(s32[1,6]{1,0:T(1,128)} %cam_len.1, s32[6,6]{1,0:T(8,128)} %view_mask.1, s32[8,8]{1,0:T(8,128)} %time_mask.1, bf16[1,384,1152]{2,1,0:T(8,128)(2,1)} %video.1, f32[1152]{0:T(1024)} %s_gain.1, f32[1152]{0:T(1024)} %t_gain.1, f32[4,72]{1,0:T(4,128)} %qk_gain.1, bf16[1728,1152]{1,0:T(8,128)(2,1)} %bitcast.2, ...), custom_call_target="tpu_custom_call" | custom-call | flops 6000000000 | bytes 13000000 | tf_op jit(solution)/shard_map/pallas_call | solution.py:458
  47.0 2.1 %copy.13 = bf16[1,384,1152]{2,1,0:T(8,128)(2,1)} copy(bf16[1,384,1152]{2,1,0:T(8,128)(2,1)} %shard_map.109) | data formatting | bytes 1769472

commit v4 on v3

--- a/solution.py
+++ b/solution.py
@@ -27,21 +27,13 @@
     return (centred * lax.rsqrt(spread + EPS) * gain).astype(BF16)
 
 
-def split_sum(values, table):
-    high = values.astype(BF16)
-    low = (values - high.astype(F32)).astype(BF16)
-    return jnp.dot(high, table, preferred_element_type=F32) + jnp.dot(
-        low, table, preferred_element_type=F32
-    )
-
-
 def project(rows, weight, gain, sums, spreads, q_ref, k_ref, v_ref, at):
     width = HEADS * HD
     packed = lax.dot_general(
         rows, weight[...], (((1,), (1,)), ((), ())), preferred_element_type=F32
     )
     qk = packed[:, : 2 * width]
-    total = split_sum(qk * qk, sums[...])
+    total = jnp.dot((qk * qk).astype(BF16), sums[...], preferred_element_type=F32)
     inverse = lax.rsqrt(total * (1.0 / HD) + EPS)
     high = inverse.astype(BF16).astype(F32)
     lane = lax.broadcasted_iota(I32, inverse.shape, 1)
@@ -187,7 +179,7 @@
         sending[at, :] = normalize(video[0, at, :].astype(F32), s_gain[...][None, :])
         return carry
 
-    lax.fori_loop(0, slots // 64, to_normed, 0)
+    lax.fori_loop(0, slots // 64, to_normed, 0, unroll=True)
     loads[0].wait()
     for load in loads[1:]:
         load.start()

time: 49.3 us -> 48.7 us (0.988)
  Pallas kernels: 47 us -> 46.3 us
    pallas_call x1, Pallas kernels: 47 us -> 46.3 us  [body(): pl.pallas_call(functools.partial(kernel, n), out_shape=jax.ShapeDtypeStru...]
where the time goes in v4:
time: 48.7 us; the launch traced here: 48.5 us
  Pallas kernels  46.3 us (95%)
  local copies, waits for them, and re-layouts  2.15 us (4%)
    pallas_call x1, Pallas kernels, body(): pl.pallas_call(functools.partial(kernel, n), out_shape=jax.ShapeDtypeStru...  46.3 us
    unnamed x1, local copies, waits for them, and re-layouts  2.15 us

profile of v4, /device:TPU:0, one launch (start us, length us, event | category | flops | bytes accessed | tf_op | source)
XLA Modules:
  0.0 48.5 jit_solution(7994646068303773765)
XLA Ops:
  0.0 46.3 %shard_map.109 = bf16[1,384,1152]{2,1,0:T(8,128)(2,1)} custom-call(s32[1,6]{1,0:T(1,128)} %cam_len.1, s32[6,6]{1,0:T(8,128)} %view_mask.1, s32[8,8]{1,0:T(8,128)} %time_mask.1, bf16[1,384,1152]{2,1,0:T(8,128)(2,1)} %video.1, f32[1152]{0:T(1024)} %s_gain.1, f32[1152]{0:T(1024)} %t_gain.1, f32[4,72]{1,0:T(4,128)} %qk_gain.1, bf16[1728,1152]{1,0:T(8,128)(2,1)} %bitcast.2, ...), custom_call_target="tpu_custom_call" | custom-call | flops 6000000000 | bytes 13000000 | tf_op jit(solution)/shard_map/pallas_call | solution.py:450
  46.3 2.1 %copy.13 = bf16[1,384,1152]{2,1,0:T(8,128)(2,1)} copy(bf16[1,384,1152]{2,1,0:T(8,128)(2,1)} %shard_map.109) | data formatting | bytes 1769472
